TPU v7x, 1024 devices: a whole 4x4x32 slice. The times are simulated.
1024 devices in a mesh: gx: 8 (over z_lo), gy: 64 (over z_hi, y, x), gz: 2 (over core).
Axes of the slice: x: 4, y: 4, z: 32 (z_hi: 4, z_lo: 8; z = z_hi * 8 + z_lo), core: 2. Of those that a mesh axis runs over, the one named last changes fastest.
Arguments:
- density: float32 [32, 512, 256], P('gx', 'gy', 'gz'), may hold values from 0.5 to 2
- velocity: float32 [3, 32, 512, 256], P(None, 'gx', 'gy', 'gz'), may hold values from -0.5 to 0.5
- magnetic: float32 [3, 32, 512, 256], P(None, 'gx', 'gy', 'gz'), may hold values from -1 to 1
- concentration: float32 [32, 512, 256], P('gx', 'gy', 'gz'), may hold values from 0 to 1
- shear_cells: int32 [2], replicated, may hold values from 0 to 511
- shear_frac: float32 [2], replicated, may hold values from 0 to 1
Outputs:
- evolved: float32 [8, 32, 512, 256], P(None, 'gx', 'gy', 'gz')
All inputs are finite; a program needn't handle non-finite values.
Results may differ from a plain program's by a relative error of at most 0.0003.
Values sent between devices are 32-bit elements; how exact they have to be, the bound alone decides.
No kernel may reach another device: no remote copies, remote signals or barrier semaphores. Data moves between devices by JAX's collectives and lax.ppermute only.
A program may use at most 32 MiB of HBM per device.

v0:
```python
import jax
import jax.numpy as jnp
from jax import lax
from jax.sharding import PartitionSpec as P

SOUND_SQUARED = 1.0
COURANT = 0.045
SHEAR_SPEED = 1.0


def extended(shard, sides, width):
    for axis, dim in sides:
        peers, length = (lax.axis_size(axis), shard.shape[dim])
        up = [(i, (i + 1) % peers) for i in range(peers)]
        down = [(j, i) for i, j in up]
        last = lax.slice_in_dim(shard, length - width, length, axis=dim)
        leading = lax.slice_in_dim(shard, 0, width, axis=dim)
        before = lax.ppermute(last, axis, up)
        after = lax.ppermute(leading, axis, down)
        shard = jnp.concatenate([before, shard, after], axis=dim)
    return shard


def shifted_2(block, axis, distance):
    devices = range(lax.axis_size(axis))
    route = [((i - distance) % len(devices), i) for i in devices]
    return lax.ppermute(block, axis, route)


def minmod_slopes(backward, forward):
    return jnp.where(
        backward * forward > 0.0,
        jnp.sign(backward) * jnp.minimum(jnp.abs(backward), jnp.abs(forward)),
        0.0,
    )


def physical_flux(conserved, normal):
    density = conserved[0]
    momentum = conserved[1:4]
    magnetic = conserved[4:7]
    velocity = momentum / density
    normal_vel = velocity[normal]
    normal_mag = magnetic[normal]
    magnetic_sq = jnp.sum(magnetic * magnetic, axis=0)
    total_press = SOUND_SQUARED * density + 0.5 * magnetic_sq
    momentum_flux = momentum * normal_vel - magnetic * normal_mag
    momentum_flux = momentum_flux.at[normal].add(total_press)
    magnetic_flux = magnetic * normal_vel - velocity * normal_mag
    fluxes = jnp.concatenate(
        [momentum[normal][None], momentum_flux, magnetic_flux, (conserved[7] * normal_vel)[None]],
        axis=0,
    )
    speeds = jnp.abs(normal_vel) + jnp.sqrt(SOUND_SQUARED + magnetic_sq / density)
    return (fluxes, speeds)


def cell_range(padded, offset, length, axis_dim):
    return lax.slice_in_dim(padded, offset, offset + length, axis=axis_dim)


def flux_difference(padded, axis_dim, normal):
    inner_count = padded.shape[axis_dim] - 4
    center = cell_range(padded, 1, inner_count + 2, axis_dim)
    slopes = minmod_slopes(
        center - cell_range(padded, 0, inner_count + 2, axis_dim),
        cell_range(padded, 2, inner_count + 2, axis_dim) - center,
    )
    upper_face = center + 0.5 * slopes
    lower_face = center - 0.5 * slopes
    left_state = cell_range(upper_face, 0, inner_count + 1, axis_dim)
    right_state = cell_range(lower_face, 1, inner_count + 1, axis_dim)
    left_flux, left_speed = physical_flux(left_state, normal)
    right_flux, right_speed = physical_flux(right_state, normal)
    fluxes = 0.5 * (left_flux + right_flux) - 0.5 * jnp.maximum(left_speed, right_speed) * (
        right_state - left_state
    )
    return cell_range(fluxes, 1, inner_count, axis_dim) - cell_range(
        fluxes, 0, inner_count, axis_dim
    )


def lagrange_weights(fraction):
    node_list = (-1, 0, 1, 2)
    weights = []
    for target in node_list:
        weight = jnp.ones((), fraction.dtype)
        for source in node_list:
            if source != target:
                weight = weight * (source - fraction) / (source - target)
        weights.append(weight)
    return weights


def widen_strip(face_strip, width):
    return extended(face_strip, (("gy", 2),), width)


def advance_strip(face_strip, blocks):
    for position in range((lax.axis_size("gy") - 1).bit_length()):
        shifted = shifted_2(face_strip, "gy", 1 << position)
        face_strip = jnp.where((blocks >> position) % 2 == 1, shifted, face_strip)
    return face_strip


def sheared_ghosts(padded_x, shift_cells, fraction):
    block_y = padded_x.shape[2]
    row_index = lax.axis_index("gx")
    is_first = row_index == 0
    is_last = row_index == lax.axis_size("gx") - 1
    total_y = block_y * lax.axis_size("gy")
    offsets = jnp.where(is_first, shift_cells, total_y - shift_cells - 1)
    reach_cells = offsets + 2
    blocks = reach_cells // block_y % lax.axis_size("gy")
    within = reach_cells % block_y
    face_strip = jnp.where(is_first, padded_x[:, :2], padded_x[:, -2:])
    arrived = advance_strip(widen_strip(face_strip, block_y), blocks)
    window = lax.dynamic_slice_in_dim(arrived, block_y - within, block_y + 3, axis=2)
    weights = lagrange_weights(fraction)
    ghost_layers = jnp.zeros_like(face_strip)
    for position in range(4):
        factor = jnp.where(is_first, weights[position], weights[3 - position])
        ghost_layers = ghost_layers + factor * window[:, :, 3 - position : 3 - position + block_y]
    ghost_layers = ghost_layers.at[2].add(
        jnp.where(is_first, SHEAR_SPEED, -SHEAR_SPEED) * ghost_layers[0]
    )
    lower_side = jnp.where(is_first, ghost_layers, padded_x[:, :2])
    upper_side = jnp.where(is_last, ghost_layers, padded_x[:, -2:])
    return jnp.concatenate([lower_side, padded_x[:, 2:-2], upper_side], axis=1)


def section_rate(conserved, shift_cells, fraction):
    padded = extended(conserved, (("gx", 1), ("gy", 2), ("gz", 3)), 2)
    vertical = flux_difference(padded[:, 2:-2, 2:-2, :], 3, 2)
    azimuthal = flux_difference(padded[:, 2:-2, :, 2:-2], 2, 1)
    radial = flux_difference(sheared_ghosts(padded[:, :, 2:-2, 2:-2], shift_cells, fraction), 1, 0)
    return -(radial + azimuthal + vertical)


def body(density, velocity, magnetic, concentration, shear_cells, shear_frac):
    initial = jnp.concatenate(
        [density[None], density[None] * velocity, magnetic, (density * concentration)[None]], axis=0
    )
    midway = initial + COURANT * section_rate(initial, shear_cells[0], shear_frac[0])
    return 0.5 * initial + 0.5 * (
        midway + COURANT * section_rate(midway, shear_cells[1], shear_frac[1])
    )


def solution(mesh):
    placed = (
        P("gx", "gy", "gz"),
        P(None, "gx", "gy", "gz"),
        P(None, "gx", "gy", "gz"),
        P("gx", "gy", "gz"),
        P(),
        P(),
    )
    return jax.shard_map(
        body, mesh=mesh, in_specs=placed, out_specs=P(None, "gx", "gy", "gz"), check_vma=False
    )
```

profile of v0, /device:TPU:64, one launch (start us, length us, event | category | flops | bytes accessed | tf_op | source)
XLA Modules:
  0.0 607.2 jit_solution(15838930324925471094)
XLA Ops:
  2.3 3.8 collective-permute-start
  14.8 3.4 collective-permute-start.2
  18.2 24.4 %collective-permute-start.3 = (f32[8,2,8,128]{3,2,1,0:T(8,128)S(1)}, f32[8,2,8,128]{3,2,1,0:T(8,128)S(1)}, u32[]{:S(2)}, u32[]{:S(2)}) collective-permute-start(f32[8,2,8,128]{3,2,1,0:T(8,128)S(1)} %broadcast_select_fusion.15), channel_id=1, source_target_pairs={{2,0},{4,2},{6,4},{8,6},{10,8},{12,10},{14,12},{16,14},{18,16},{20... | collective-permute-start | bytes 196616 | tf_op jit(solution)/shard_map/ppermute | solution.py:19
  44.6 16.9 %collective-permute-start.11 = (f32[8,8,2,128]{3,2,1,0:T(2,128)S(1)}, f32[8,8,2,128]{3,2,1,0:T(2,128)S(1)}, u32[]{:S(2)}, u32[]{:S(2)}) collective-permute-start(f32[8,8,2,128]{3,2,1,0:T(2,128)S(1)} %get-tuple-element.260), channel_id=1, source_target_pairs={{2,0},{4,2},{6,4},{8,6},{10,8},{12,10},{14,12},{16,14},{18,16},{20... | collective-permute-start | bytes 196616 | tf_op jit(solution)/shard_map/ppermute | solution.py:19
  73.1 16.6 %collective-permute-done.4 = f32[8,2,24,128]{3,2,1,0:T(8,128)S(1)} collective-permute-done((f32[8,2,24,128]{3,2,1,0:T(8,128)S(1)}, f32[8,2,24,128]{3,2,1,0:T(8,128)S(1)}, u32[]{:S(2)}, u32[]{:S(2)}) %collective-permute-start.4) | collective-permute-done | bytes 196640 | tf_op jit(solution)/shard_map/ppermute | solution.py:27
  91.6 27.5 %collective-permute-done.5 = f32[8,2,24,128]{3,2,1,0:T(8,128)S(1)} collective-permute-done((f32[8,2,24,128]{3,2,1,0:T(8,128)S(1)}, f32[8,2,24,128]{3,2,1,0:T(8,128)S(1)}, u32[]{:S(2)}, u32[]{:S(2)}) %collective-permute-start.5) | collective-permute-done | bytes 196640 | tf_op jit(solution)/shard_map/ppermute | solution.py:27
  121.1 17.4 %collective-permute-done.6 = f32[8,2,24,128]{3,2,1,0:T(8,128)S(1)} collective-permute-done((f32[8,2,24,128]{3,2,1,0:T(8,128)S(1)}, f32[8,2,24,128]{3,2,1,0:T(8,128)S(1)}, u32[]{:S(2)}, u32[]{:S(2)}) %collective-permute-start.6) | collective-permute-done | bytes 196640 | tf_op jit(solution)/shard_map/ppermute | solution.py:27
  140.6 16.6 %collective-permute-done.7 = f32[8,2,24,128]{3,2,1,0:T(8,128)S(1)} collective-permute-done((f32[8,2,24,128]{3,2,1,0:T(8,128)S(1)}, f32[8,2,24,128]{3,2,1,0:T(8,128)S(1)}, u32[]{:S(2)}, u32[]{:S(2)}) %collective-permute-start.7) | collective-permute-done | bytes 196640 | tf_op jit(solution)/shard_map/ppermute | solution.py:27
  157.3 3.8 collective-permute-start.8
  161.2 12.4 %collective-permute-done.8 = f32[8,2,24,128]{3,2,1,0:T(8,128)S(1)} collective-permute-done((f32[8,2,24,128]{3,2,1,0:T(8,128)S(1)}, f32[8,2,24,128]{3,2,1,0:T(8,128)S(1)}, u32[]{:S(2)}, u32[]{:S(2)}) %collective-permute-start.8) | collective-permute-done | bytes 196640 | tf_op jit(solution)/shard_map/ppermute | solution.py:27
  173.6 4.7 collective-permute-start.9
  178.4 23.1 %collective-permute-done.9 = f32[8,2,24,128]{3,2,1,0:T(8,128)S(1)} collective-permute-done((f32[8,2,24,128]{3,2,1,0:T(8,128)S(1)}, f32[8,2,24,128]{3,2,1,0:T(8,128)S(1)}, u32[]{:S(2)}, u32[]{:S(2)}) %collective-permute-start.9) | collective-permute-done | bytes 196640 | tf_op jit(solution)/shard_map/ppermute | solution.py:27
  202.3 15.8 %collective-permute-start.14 = (f32[8,2,8,128]{3,2,1,0:T(8,128)S(1)}, f32[8,2,8,128]{3,2,1,0:T(8,128)S(1)}, u32[]{:S(2)}, u32[]{:S(2)}) collective-permute-start(f32[8,2,8,128]{3,2,1,0:T(8,128)S(1)} %get-tuple-element.295), channel_id=1, source_target_pairs={{0,128},{128,256},{256,384},{384,512},{512,640},{640,768},{768,896... | collective-permute-start | bytes 196616 | tf_op jit(solution)/shard_map/ppermute | solution.py:18
  218.1 99.7 %collective-permute-start.15 = (f32[8,2,8,128]{3,2,1,0:T(8,128)S(1)}, f32[8,2,8,128]{3,2,1,0:T(8,128)S(1)}, u32[]{:S(2)}, u32[]{:S(2)}) collective-permute-start(f32[8,2,8,128]{3,2,1,0:T(8,128)S(1)} %get-tuple-element.296), channel_id=1, source_target_pairs={{128,0},{256,128},{384,256},{512,384},{640,512},{768,640},{896,768... | collective-permute-start | bytes 196616 | tf_op jit(solution)/shard_map/ppermute | solution.py:19
  323.4 16.9 %collective-permute-start.17 = (f32[8,2,8,128]{3,2,1,0:T(8,128)S(1)}, f32[8,2,8,128]{3,2,1,0:T(8,128)S(1)}, u32[]{:S(2)}, u32[]{:S(2)}) collective-permute-start(f32[8,2,8,128]{3,2,1,0:T(8,128)S(1)} %broadcast_select_fusion.13), channel_id=1, source_target_pairs={{2,0},{4,2},{6,4},{8,6},{10,8},{12,10},{14,12},{16,14},{18,16},{20... | collective-permute-start | bytes 196616 | tf_op jit(solution)/shard_map/ppermute | solution.py:19
  342.2 16.9 %collective-permute-start.25 = (f32[8,8,2,128]{3,2,1,0:T(2,128)S(1)}, f32[8,8,2,128]{3,2,1,0:T(2,128)S(1)}, u32[]{:S(2)}, u32[]{:S(2)}) collective-permute-start(f32[8,8,2,128]{3,2,1,0:T(2,128)S(1)} %get-tuple-element.242), channel_id=1, source_target_pairs={{2,0},{4,2},{6,4},{8,6},{10,8},{12,10},{14,12},{16,14},{18,16},{20... | collective-permute-start | bytes 196616 | tf_op jit(solution)/shard_map/ppermute | solution.py:19
  368.2 117.8 %collective-permute-done.18 = f32[8,2,24,128]{3,2,1,0:T(8,128)S(1)} collective-permute-done((f32[8,2,24,128]{3,2,1,0:T(8,128)S(1)}, f32[8,2,24,128]{3,2,1,0:T(8,128)S(1)}, u32[]{:S(2)}, u32[]{:S(2)}) %collective-permute-start.18) | collective-permute-done | bytes 196640 | tf_op jit(solution)/shard_map/ppermute | solution.py:27
  488.1 32.9 %collective-permute-done.19 = f32[8,2,24,128]{3,2,1,0:T(8,128)S(1)} collective-permute-done((f32[8,2,24,128]{3,2,1,0:T(8,128)S(1)}, f32[8,2,24,128]{3,2,1,0:T(8,128)S(1)}, u32[]{:S(2)}, u32[]{:S(2)}) %collective-permute-start.19) | collective-permute-done | bytes 196640 | tf_op jit(solution)/shard_map/ppermute | solution.py:27
  523.0 17.4 %collective-permute-done.20 = f32[8,2,24,128]{3,2,1,0:T(8,128)S(1)} collective-permute-done((f32[8,2,24,128]{3,2,1,0:T(8,128)S(1)}, f32[8,2,24,128]{3,2,1,0:T(8,128)S(1)}, u32[]{:S(2)}, u32[]{:S(2)}) %collective-permute-start.20) | collective-permute-done | bytes 196640 | tf_op jit(solution)/shard_map/ppermute | solution.py:27
  542.4 18.7 %collective-permute-done.21 = f32[8,2,24,128]{3,2,1,0:T(8,128)S(1)} collective-permute-done((f32[8,2,24,128]{3,2,1,0:T(8,128)S(1)}, f32[8,2,24,128]{3,2,1,0:T(8,128)S(1)}, u32[]{:S(2)}, u32[]{:S(2)}) %collective-permute-start.21) | collective-permute-done | bytes 196640 | tf_op jit(solution)/shard_map/ppermute | solution.py:27
  561.1 5.6 collective-permute-start.22
  566.9 12.2 %collective-permute-done.22 = f32[8,2,24,128]{3,2,1,0:T(8,128)S(1)} collective-permute-done((f32[8,2,24,128]{3,2,1,0:T(8,128)S(1)}, f32[8,2,24,128]{3,2,1,0:T(8,128)S(1)}, u32[]{:S(2)}, u32[]{:S(2)}) %collective-permute-start.22) | collective-permute-done | bytes 196640 | tf_op jit(solution)/shard_map/ppermute | solution.py:27
  579.1 15.3 %collective-permute-start.23 = (f32[8,2,24,128]{3,2,1,0:T(8,128)S(1)}, f32[8,2,24,128]{3,2,1,0:T(8,128)S(1)}, u32[]{:S(2)}, u32[]{:S(2)}) collective-permute-start(f32[8,2,24,128]{3,2,1,0:T(8,128)S(1)} %broadcast_select_fusion.4), channel_id=1, source_target_pairs={{64,0},{66,2},{68,4},{70,6},{72,8},{74,10},{76,12},{78,14},{80,16}... | collective-permute-start | bytes 589832 | tf_op jit(solution)/shard_map/ppermute | solution.py:27
  594.6 11.3 %collective-permute-done.23 = f32[8,2,24,128]{3,2,1,0:T(8,128)S(1)} collective-permute-done((f32[8,2,24,128]{3,2,1,0:T(8,128)S(1)}, f32[8,2,24,128]{3,2,1,0:T(8,128)S(1)}, u32[]{:S(2)}, u32[]{:S(2)}) %collective-permute-start.23) | collective-permute-done | bytes 196640 | tf_op jit(solution)/shard_map/ppermute | solution.py:27
  (152 shorter events, 47.7 us)
Async XLA Ops:
  2.3 12.5 %collective-permute-start = (f32[8,2,8,128]{3,2,1,0:T(8,128)}, f32[8,2,8,128]{3,2,1,0:T(8,128)S(1)}, u32[]{:S(2)}, u32[]{:S(2)}) collective-permute-start(f32[8,2,8,128]{3,2,1,0:T(8,128)} %get-tuple-element.299), channel_id=1, source_target_pairs={{0,128},{128,256},{256,384},{384,512},{512,640},{640,768},{768,896... | collective-permute-start | bytes 196616 | tf_op jit(solution)/shard_map/ppermute | solution.py:18
  6.1 8.7 %collective-permute-start.1 = (f32[8,2,8,128]{3,2,1,0:T(8,128)}, f32[8,2,8,128]{3,2,1,0:T(8,128)S(1)}, u32[]{:S(2)}, u32[]{:S(2)}) collective-permute-start(f32[8,2,8,128]{3,2,1,0:T(8,128)} %get-tuple-element.300), channel_id=1, source_target_pairs={{128,0},{256,128},{384,256},{512,384},{640,512},{768,640},{896,768... | collective-permute-start | bytes 196616 | tf_op jit(solution)/shard_map/ppermute | solution.py:19
  14.8 46.7 %collective-permute-start.2 = (f32[8,2,8,128]{3,2,1,0:T(8,128)S(1)}, f32[8,2,8,128]{3,2,1,0:T(8,128)S(1)}, u32[]{:S(2)}, u32[]{:S(2)}) collective-permute-start(f32[8,2,8,128]{3,2,1,0:T(8,128)S(1)} %broadcast_select_fusion.15), channel_id=1, source_target_pairs={{0,2},{2,4},{4,6},{6,8},{8,10},{10,12},{12,14},{14,16},{16,18},{18... | collective-permute-start | bytes 196616 | tf_op jit(solution)/shard_map/ppermute | solution.py:18
  18.2 43.3 %collective-permute-start.3 = (f32[8,2,8,128]{3,2,1,0:T(8,128)S(1)}, f32[8,2,8,128]{3,2,1,0:T(8,128)S(1)}, u32[]{:S(2)}, u32[]{:S(2)}) collective-permute-start(f32[8,2,8,128]{3,2,1,0:T(8,128)S(1)} %broadcast_select_fusion.15), channel_id=1, source_target_pairs={{2,0},{4,2},{6,4},{8,6},{10,8},{12,10},{14,12},{16,14},{18,16},{20... | collective-permute-start | bytes 196616 | tf_op jit(solution)/shard_map/ppermute | solution.py:19
  42.7 20.8 %collective-permute-start.10 = (f32[8,8,2,128]{3,2,1,0:T(2,128)S(1)}, f32[8,8,2,128]{3,2,1,0:T(2,128)S(1)}, u32[]{:S(2)}, u32[]{:S(2)}) collective-permute-start(f32[8,8,2,128]{3,2,1,0:T(2,128)S(1)} %get-tuple-element.259), channel_id=1, source_target_pairs={{0,2},{2,4},{4,6},{6,8},{8,10},{10,12},{12,14},{14,16},{16,18},{18... | collective-permute-start | bytes 196616 | tf_op jit(solution)/shard_map/ppermute | solution.py:18
  44.6 21.2 %collective-permute-start.11 = (f32[8,8,2,128]{3,2,1,0:T(2,128)S(1)}, f32[8,8,2,128]{3,2,1,0:T(2,128)S(1)}, u32[]{:S(2)}, u32[]{:S(2)}) collective-permute-start(f32[8,8,2,128]{3,2,1,0:T(2,128)S(1)} %get-tuple-element.260), channel_id=1, source_target_pairs={{2,0},{4,2},{6,4},{8,6},{10,8},{12,10},{14,12},{16,14},{18,16},{20... | collective-permute-start | bytes 196616 | tf_op jit(solution)/shard_map/ppermute | solution.py:19
  61.5 28.1 %collective-permute-start.4 = (f32[8,2,24,128]{3,2,1,0:T(8,128)S(1)}, f32[8,2,24,128]{3,2,1,0:T(8,128)S(1)}, u32[]{:S(2)}, u32[]{:S(2)}) collective-permute-start(f32[8,2,24,128]{3,2,1,0:T(8,128)S(1)} %pad_maximum_fusion.61), channel_id=1, source_target_pairs={{126,0},{0,2},{2,4},{4,6},{6,8},{8,10},{10,12},{12,14},{14,16},{16... | collective-permute-start | bytes 589832 | tf_op jit(solution)/shard_map/ppermute | solution.py:27
  89.7 29.5 %collective-permute-start.5 = (f32[8,2,24,128]{3,2,1,0:T(8,128)S(1)}, f32[8,2,24,128]{3,2,1,0:T(8,128)S(1)}, u32[]{:S(2)}, u32[]{:S(2)}) collective-permute-start(f32[8,2,24,128]{3,2,1,0:T(8,128)S(1)} %broadcast_select_fusion.5), channel_id=1, source_target_pairs={{124,0},{126,2},{0,4},{2,6},{4,8},{6,10},{8,12},{10,14},{12,16},{1... | collective-permute-start | bytes 589832 | tf_op jit(solution)/shard_map/ppermute | solution.py:27
  119.2 19.3 %collective-permute-start.6 = (f32[8,2,24,128]{3,2,1,0:T(8,128)S(1)}, f32[8,2,24,128]{3,2,1,0:T(8,128)S(1)}, u32[]{:S(2)}, u32[]{:S(2)}) collective-permute-start(f32[8,2,24,128]{3,2,1,0:T(8,128)S(1)} %broadcast_select_fusion.6), channel_id=1, source_target_pairs={{120,0},{122,2},{124,4},{126,6},{0,8},{2,10},{4,12},{6,14},{8,16},... | collective-permute-start | bytes 589832 | tf_op jit(solution)/shard_map/ppermute | solution.py:27
  138.5 18.7 %collective-permute-start.7 = (f32[8,2,24,128]{3,2,1,0:T(8,128)S(1)}, f32[8,2,24,128]{3,2,1,0:T(8,128)S(1)}, u32[]{:S(2)}, u32[]{:S(2)}) collective-permute-start(f32[8,2,24,128]{3,2,1,0:T(8,128)S(1)} %broadcast_select_fusion.7), channel_id=1, source_target_pairs={{112,0},{114,2},{116,4},{118,6},{120,8},{122,10},{124,12},{126,14}... | collective-permute-start | bytes 589832 | tf_op jit(solution)/shard_map/ppermute | solution.py:27
  157.3 16.3 %collective-permute-start.8 = (f32[8,2,24,128]{3,2,1,0:T(8,128)S(1)}, f32[8,2,24,128]{3,2,1,0:T(8,128)S(1)}, u32[]{:S(2)}, u32[]{:S(2)}) collective-permute-start(f32[8,2,24,128]{3,2,1,0:T(8,128)S(1)} %broadcast_select_fusion.8), channel_id=1, source_target_pairs={{96,0},{98,2},{100,4},{102,6},{104,8},{106,10},{108,12},{110,14},{... | collective-permute-start | bytes 589832 | tf_op jit(solution)/shard_map/ppermute | solution.py:27
  173.6 27.9 %collective-permute-start.9 = (f32[8,2,24,128]{3,2,1,0:T(8,128)S(1)}, f32[8,2,24,128]{3,2,1,0:T(8,128)S(1)}, u32[]{:S(2)}, u32[]{:S(2)}) collective-permute-start(f32[8,2,24,128]{3,2,1,0:T(8,128)S(1)} %broadcast_select_fusion.9), channel_id=1, source_target_pairs={{64,0},{66,2},{68,4},{70,6},{72,8},{74,10},{76,12},{78,14},{80,16}... | collective-permute-start | bytes 589832 | tf_op jit(solution)/shard_map/ppermute | solution.py:27
  202.3 119.2 %collective-permute-start.14 = (f32[8,2,8,128]{3,2,1,0:T(8,128)S(1)}, f32[8,2,8,128]{3,2,1,0:T(8,128)S(1)}, u32[]{:S(2)}, u32[]{:S(2)}) collective-permute-start(f32[8,2,8,128]{3,2,1,0:T(8,128)S(1)} %get-tuple-element.295), channel_id=1, source_target_pairs={{0,128},{128,256},{256,384},{384,512},{512,640},{640,768},{768,896... | collective-permute-start | bytes 196616 | tf_op jit(solution)/shard_map/ppermute | solution.py:18
  218.1 103.3 %collective-permute-start.15 = (f32[8,2,8,128]{3,2,1,0:T(8,128)S(1)}, f32[8,2,8,128]{3,2,1,0:T(8,128)S(1)}, u32[]{:S(2)}, u32[]{:S(2)}) collective-permute-start(f32[8,2,8,128]{3,2,1,0:T(8,128)S(1)} %get-tuple-element.296), channel_id=1, source_target_pairs={{128,0},{256,128},{384,256},{512,384},{640,512},{768,640},{896,768... | collective-permute-start | bytes 196616 | tf_op jit(solution)/shard_map/ppermute | solution.py:19
  321.5 37.6 %collective-permute-start.16 = (f32[8,2,8,128]{3,2,1,0:T(8,128)S(1)}, f32[8,2,8,128]{3,2,1,0:T(8,128)S(1)}, u32[]{:S(2)}, u32[]{:S(2)}) collective-permute-start(f32[8,2,8,128]{3,2,1,0:T(8,128)S(1)} %broadcast_select_fusion.13), channel_id=1, source_target_pairs={{0,2},{2,4},{4,6},{6,8},{8,10},{10,12},{12,14},{14,16},{16,18},{18... | collective-permute-start | bytes 196616 | tf_op jit(solution)/shard_map/ppermute | solution.py:18
  323.4 35.7 %collective-permute-start.17 = (f32[8,2,8,128]{3,2,1,0:T(8,128)S(1)}, f32[8,2,8,128]{3,2,1,0:T(8,128)S(1)}, u32[]{:S(2)}, u32[]{:S(2)}) collective-permute-start(f32[8,2,8,128]{3,2,1,0:T(8,128)S(1)} %broadcast_select_fusion.13), channel_id=1, source_target_pairs={{2,0},{4,2},{6,4},{8,6},{10,8},{12,10},{14,12},{16,14},{18,16},{20... | collective-permute-start | bytes 196616 | tf_op jit(solution)/shard_map/ppermute | solution.py:19
  340.3 20.8 %collective-permute-start.24 = (f32[8,8,2,128]{3,2,1,0:T(2,128)S(1)}, f32[8,8,2,128]{3,2,1,0:T(2,128)S(1)}, u32[]{:S(2)}, u32[]{:S(2)}) collective-permute-start(f32[8,8,2,128]{3,2,1,0:T(2,128)S(1)} %get-tuple-element.241), channel_id=1, source_target_pairs={{0,2},{2,4},{4,6},{6,8},{8,10},{10,12},{12,14},{14,16},{16,18},{18... | collective-permute-start | bytes 196616 | tf_op jit(solution)/shard_map/ppermute | solution.py:18
  342.2 18.8 %collective-permute-start.25 = (f32[8,8,2,128]{3,2,1,0:T(2,128)S(1)}, f32[8,8,2,128]{3,2,1,0:T(2,128)S(1)}, u32[]{:S(2)}, u32[]{:S(2)}) collective-permute-start(f32[8,8,2,128]{3,2,1,0:T(2,128)S(1)} %get-tuple-element.242), channel_id=1, source_target_pairs={{2,0},{4,2},{6,4},{8,6},{10,8},{12,10},{14,12},{16,14},{18,16},{20... | collective-permute-start | bytes 196616 | tf_op jit(solution)/shard_map/ppermute | solution.py:19
  359.2 126.9 %collective-permute-start.18 = (f32[8,2,24,128]{3,2,1,0:T(8,128)S(1)}, f32[8,2,24,128]{3,2,1,0:T(8,128)S(1)}, u32[]{:S(2)}, u32[]{:S(2)}) collective-permute-start(f32[8,2,24,128]{3,2,1,0:T(8,128)S(1)} %pad_maximum_fusion.62), channel_id=1, source_target_pairs={{126,0},{0,2},{2,4},{4,6},{6,8},{8,10},{10,12},{12,14},{14,16},{16... | collective-permute-start | bytes 589832 | tf_op jit(solution)/shard_map/ppermute | solution.py:27
  486.1 34.9 %collective-permute-start.19 = (f32[8,2,24,128]{3,2,1,0:T(8,128)S(1)}, f32[8,2,24,128]{3,2,1,0:T(8,128)S(1)}, u32[]{:S(2)}, u32[]{:S(2)}) collective-permute-start(f32[8,2,24,128]{3,2,1,0:T(8,128)S(1)} %broadcast_select_fusion), channel_id=1, source_target_pairs={{124,0},{126,2},{0,4},{2,6},{4,8},{6,10},{8,12},{10,14},{12,16},{1... | collective-permute-start | bytes 589832 | tf_op jit(solution)/shard_map/ppermute | solution.py:27
  521.0 19.3 %collective-permute-start.20 = (f32[8,2,24,128]{3,2,1,0:T(8,128)S(1)}, f32[8,2,24,128]{3,2,1,0:T(8,128)S(1)}, u32[]{:S(2)}, u32[]{:S(2)}) collective-permute-start(f32[8,2,24,128]{3,2,1,0:T(8,128)S(1)} %broadcast_select_fusion.1), channel_id=1, source_target_pairs={{120,0},{122,2},{124,4},{126,6},{0,8},{2,10},{4,12},{6,14},{8,16},... | collective-permute-start | bytes 589832 | tf_op jit(solution)/shard_map/ppermute | solution.py:27
  540.4 20.8 %collective-permute-start.21 = (f32[8,2,24,128]{3,2,1,0:T(8,128)S(1)}, f32[8,2,24,128]{3,2,1,0:T(8,128)S(1)}, u32[]{:S(2)}, u32[]{:S(2)}) collective-permute-start(f32[8,2,24,128]{3,2,1,0:T(8,128)S(1)} %broadcast_select_fusion.2), channel_id=1, source_target_pairs={{112,0},{114,2},{116,4},{118,6},{120,8},{122,10},{124,12},{126,14}... | collective-permute-start | bytes 589832 | tf_op jit(solution)/shard_map/ppermute | solution.py:27
  561.1 18.0 %collective-permute-start.22 = (f32[8,2,24,128]{3,2,1,0:T(8,128)S(1)}, f32[8,2,24,128]{3,2,1,0:T(8,128)S(1)}, u32[]{:S(2)}, u32[]{:S(2)}) collective-permute-start(f32[8,2,24,128]{3,2,1,0:T(8,128)S(1)} %broadcast_select_fusion.3), channel_id=1, source_target_pairs={{96,0},{98,2},{100,4},{102,6},{104,8},{106,10},{108,12},{110,14},{... | collective-permute-start | bytes 589832 | tf_op jit(solution)/shard_map/ppermute | solution.py:27
  579.1 26.8 %collective-permute-start.23 = (f32[8,2,24,128]{3,2,1,0:T(8,128)S(1)}, f32[8,2,24,128]{3,2,1,0:T(8,128)S(1)}, u32[]{:S(2)}, u32[]{:S(2)}) collective-permute-start(f32[8,2,24,128]{3,2,1,0:T(8,128)S(1)} %broadcast_select_fusion.4), channel_id=1, source_target_pairs={{64,0},{66,2},{68,4},{70,6},{72,8},{74,10},{76,12},{78,14},{80,16}... | collective-permute-start | bytes 589832 | tf_op jit(solution)/shard_map/ppermute | solution.py:27
  (9 other events, 20.9 us)
where the time goes:
time: 608 us; the launch traced here: 607 us
  waiting for transfers between devices  329 us (54%)
  starting transfers between devices  259 us (43%)
  between operations  8.47 us (1%)
  other arithmetic  6.72 us (1%)
    ppermute x12, waiting for transfers between devices, shifted_2(): return lax.ppermute(block, axis, route)  324 us
    ppermute x8, starting transfers between devices, extended(): after = lax.ppermute(leading, axis, down)  181 us
    ppermute x12, starting transfers between devices, shifted_2(): return lax.ppermute(block, axis, route)  44.8 us
    ppermute x8, starting transfers between devices, extended(): before = lax.ppermute(last, axis, up)  32.6 us
  transfers between devices with their start and end apart: 28, of which 15 were waited for; matrix products, arithmetic and copies ran while one was open for 1% of the time, Pallas kernels for 0%

commit v1 on v0

--- a/solution.py
+++ b/solution.py
@@ -6,25 +6,6 @@
 SOUND_SQUARED = 1.0
 COURANT = 0.045
 SHEAR_SPEED = 1.0
-
-
-def extended(shard, sides, width):
-    for axis, dim in sides:
-        peers, length = (lax.axis_size(axis), shard.shape[dim])
-        up = [(i, (i + 1) % peers) for i in range(peers)]
-        down = [(j, i) for i, j in up]
-        last = lax.slice_in_dim(shard, length - width, length, axis=dim)
-        leading = lax.slice_in_dim(shard, 0, width, axis=dim)
-        before = lax.ppermute(last, axis, up)
-        after = lax.ppermute(leading, axis, down)
-        shard = jnp.concatenate([before, shard, after], axis=dim)
-    return shard
-
-
-def shifted_2(block, axis, distance):
-    devices = range(lax.axis_size(axis))
-    route = [((i - distance) % len(devices), i) for i in devices]
-    return lax.ppermute(block, axis, route)
 
 
 def minmod_slopes(backward, forward):
@@ -92,48 +73,104 @@
     return weights
 
 
-def widen_strip(face_strip, width):
-    return extended(face_strip, (("gy", 2),), width)
+def by_offset(near):
+    rows, columns = lax.axis_size("gx"), lax.axis_size("gy")
+    route = []
+    for j in range(columns):
+        route.append(((rows - 1) * columns + j, (rows - 1) * columns + (j + near) % columns))
+        route.append((j, (j - near) % columns))
+    return route
 
 
-def advance_strip(face_strip, blocks):
-    for position in range((lax.axis_size("gy") - 1).bit_length()):
-        shifted = shifted_2(face_strip, "gy", 1 << position)
-        face_strip = jnp.where((blocks >> position) % 2 == 1, shifted, face_strip)
-    return face_strip
+def radial_routes(blocks):
+    rows, columns = lax.axis_size("gx"), lax.axis_size("gy")
+    up, down = [], []
+    for i in range(rows - 1):
+        for j in range(columns):
+            up.append((i * columns + j, (i + 1) * columns + j))
+            down.append(((i + 1) * columns + j, i * columns + j))
+    for j in range(columns):
+        up.append(((rows - 1) * columns + j, (j + blocks) % columns))
+        down.append((j, (rows - 1) * columns + (j - blocks) % columns))
+    return up, down
 
 
-def sheared_ghosts(padded_x, shift_cells, fraction):
-    block_y = padded_x.shape[2]
-    row_index = lax.axis_index("gx")
-    is_first = row_index == 0
-    is_last = row_index == lax.axis_size("gx") - 1
-    total_y = block_y * lax.axis_size("gy")
-    offsets = jnp.where(is_first, shift_cells, total_y - shift_cells - 1)
-    reach_cells = offsets + 2
-    blocks = reach_cells // block_y % lax.axis_size("gy")
-    within = reach_cells % block_y
-    face_strip = jnp.where(is_first, padded_x[:, :2], padded_x[:, -2:])
-    arrived = advance_strip(widen_strip(face_strip, block_y), blocks)
-    window = lax.dynamic_slice_in_dim(arrived, block_y - within, block_y + 3, axis=2)
+def near_exchange(near):
+    def branch(operands):
+        conserved, strip, pair, first_rows, last_rows = operands
+        over = ("gx", "gy")
+        beyond = lax.ppermute(strip, over, by_offset(near + 1))
+        own = lax.ppermute(strip, over, by_offset(near)) if near else strip
+        short = lax.ppermute(pair, over, by_offset(near - 1)) if near != 1 else pair
+        other = lax.ppermute(conserved, "gz", [(0, 1), (1, 0)])
+        peers = lax.axis_size("gy")
+        upward = [(i, (i + 1) % peers) for i in range(peers)]
+        before = lax.ppermute(last_rows, "gy", upward)
+        after = lax.ppermute(first_rows, "gy", [(b, a) for a, b in upward])
+        return beyond, own, short, other, before, after
+
+    return branch
+
+
+def far_exchange(blocks):
+    def branch(operands):
+        upward, downward = operands
+        up, down = radial_routes(blocks)
+        over = ("gx", "gy")
+        return lax.ppermute(upward, over, up), lax.ppermute(downward, over, down)
+
+    return branch
+
+
+def halos(conserved, shift_cells, fraction):
+    fields, layers, block_y, block_z = conserved.shape
+    columns = lax.axis_size("gy")
+    is_first = lax.axis_index("gx") == 0
+    is_last = lax.axis_index("gx") == lax.axis_size("gx") - 1
+    blocks = (shift_cells + 1) // block_y % columns
+    within = (shift_cells + 1) % block_y
+    group = 8
+    lower, upper = conserved[:, :2], conserved[:, -2:]
+    strip = jnp.where(is_first, lower, upper)
+    pair = jnp.where(is_first, strip[:, :, -2:], strip[:, :, :2]).reshape(fields, 4, block_z)
+    first_rows = conserved[:, :, :2].reshape(fields, 2 * layers, block_z)
+    last_rows = conserved[:, :, -2:].reshape(fields, 2 * layers, block_z)
+    beyond, own, short, other, before, after = lax.switch(
+        blocks % group,
+        [near_exchange(n) for n in range(group)],
+        (conserved, strip, pair, first_rows, last_rows),
+    )
+    short = short.reshape(fields, 2, 2, block_z)
+    before = before.reshape(fields, layers, 2, block_z)
+    after = after.reshape(fields, layers, 2, block_z)
+    rows = jnp.where(
+        is_first,
+        jnp.concatenate([short, own, beyond], axis=2),
+        jnp.concatenate([beyond, own, short], axis=2),
+    )
+    start = jnp.where(is_first, within, block_y - 1 - within)
+    window = lax.dynamic_slice_in_dim(rows, start, block_y + 3, axis=2)
     weights = lagrange_weights(fraction)
-    ghost_layers = jnp.zeros_like(face_strip)
+    ghost = jnp.zeros_like(strip)
     for position in range(4):
         factor = jnp.where(is_first, weights[position], weights[3 - position])
-        ghost_layers = ghost_layers + factor * window[:, :, 3 - position : 3 - position + block_y]
-    ghost_layers = ghost_layers.at[2].add(
-        jnp.where(is_first, SHEAR_SPEED, -SHEAR_SPEED) * ghost_layers[0]
+        ghost = ghost + factor * window[:, :, position : position + block_y]
+    ghost = ghost.at[2].add(jnp.where(is_first, -SHEAR_SPEED, SHEAR_SPEED) * ghost[0])
+    below, above = lax.switch(
+        blocks // group,
+        [far_exchange(group * n) for n in range(columns // group)],
+        (jnp.where(is_last, ghost, upper), jnp.where(is_first, ghost, lower)),
     )
-    lower_side = jnp.where(is_first, ghost_layers, padded_x[:, :2])
-    upper_side = jnp.where(is_last, ghost_layers, padded_x[:, -2:])
-    return jnp.concatenate([lower_side, padded_x[:, 2:-2], upper_side], axis=1)
+    return below, above, before, after, other
 
 
 def section_rate(conserved, shift_cells, fraction):
-    padded = extended(conserved, (("gx", 1), ("gy", 2), ("gz", 3)), 2)
-    vertical = flux_difference(padded[:, 2:-2, 2:-2, :], 3, 2)
-    azimuthal = flux_difference(padded[:, 2:-2, :, 2:-2], 2, 1)
-    radial = flux_difference(sheared_ghosts(padded[:, :, 2:-2, 2:-2], shift_cells, fraction), 1, 0)
+    below, above, before, after, other = halos(conserved, shift_cells, fraction)
+    vertical = flux_difference(
+        jnp.concatenate([other[..., -2:], conserved, other[..., :2]], axis=3), 3, 2
+    )
+    azimuthal = flux_difference(jnp.concatenate([before, conserved, after], axis=2), 2, 1)
+    radial = flux_difference(jnp.concatenate([below, conserved, above], axis=1), 1, 0)
     return -(radial + azimuthal + vertical)
 
 

time: 608 us -> 176 us (0.29)
  the two profiles are of different devices: /device:TPU:64 before, /device:TPU:238 now
where the time goes in v1:
time: 176 us; the launch traced here: 174 us
  starting transfers between devices  105 us (60%)
  waiting for transfers between devices  42.5 us (24%)
  other arithmetic  12.3 us (7%)
  local copies, waits for them, and re-layouts  7.18 us (4%)
  between operations  7.09 us (4%)
    ppermute x4, starting transfers between devices, branch(): return (lax.ppermute(upward, over, up), lax.ppermute(downward, over, down))  38.3 us
    ppermute x4, waiting for transfers between devices, branch(): return (lax.ppermute(upward, over, up), lax.ppermute(downward, over, down))  38.1 us
    ppermute x2, starting transfers between devices, branch(): own = lax.ppermute(strip, over, by_offset(near)) if near else strip  33 us
    ppermute x2, starting transfers between devices, branch(): beyond = lax.ppermute(strip, over, by_offset(near + 1))  12.5 us
    ppermute x2, starting transfers between devices, branch(): before = lax.ppermute(last_rows, 'gy', upward)  6.24 us
    ppermute x2, starting transfers between devices, branch(): after = lax.ppermute(first_rows, 'gy', [(b, a) for a, b in upward])  5.84 us
    ppermute x1, starting transfers between devices, branch(): short = lax.ppermute(pair, over, by_offset(near - 1)) if near != 1 else pair  4.99 us
    sub x6, other arithmetic, flux_difference(): lower_face = center - 0.5 * slopes  4.85 us
  transfers between devices with their start and end apart: 15, of which 5 were waited for; matrix products, arithmetic and copies ran while one was open for 2% of the time, Pallas kernels for 0%

profile of v1, /device:TPU:238, one launch (start us, length us, event | category | flops | bytes accessed | tf_op | source)
XLA Modules:
  0.0 174.2 jit_solution(10704664434351909571)
XLA Ops:
  0.0 1.3 fusion.158
  4.3 37.3 %conditional.4 = (f32[8,2,8,128]{3,2,1,0:T(8,128)}, f32[8,2,8,128]{3,2,1,0:T(8,128)S(1)}, f32[8,4,8,128]{3,2,1,0:T(8,128)}, f32[8,2,2,128]{3,2,1,0:T(2,128)}, f3...) conditional(s32[]{:T(128)} %clamp.13, ...), branch_computations={%region_0.1_spmd, %region_1.2_spmd, %region_2.3_spmd, %region_3.4_... | conditional | bytes 1777996 | solution.py:138
  4.4 1.9 %collective-permute-start.74 = (f32[8,4,8,128]{3,2,1,0:T(8,128)S(1)}, f32[8,4,8,128]{3,2,1,0:T(8,128)}, u32[]{:S(2)}, u32[]{:S(2)}) collective-permute-start(f32[8,4,8,128]{3,2,1,0:T(8,128)S(1)} %get-tuple-element.699), channel_id=1, source_target_pairs={{0,1},{1,0},{2,3},{3,2},{4,5},{5,4},{6,7},{7,6},{8,9},{9,8},{10,11... | collective-permute-start | bytes 393224 | tf_op jit(solution)/shard_map/cond/branch_7_fun/ppermute | solution.py:105
  6.3 4.2 %collective-permute-start.72 = (f32[8,2,8,128]{3,2,1,0:T(8,128)S(1)}, f32[8,2,8,128]{3,2,1,0:T(8,128)S(1)}, u32[]{:S(2)}, u32[]{:S(2)}) collective-permute-start(f32[8,2,8,128]{3,2,1,0:T(8,128)S(1)} %get-tuple-element.698), channel_id=1, source_target_pairs={{896,912},{0,112},{898,914},{2,114},{900,916},{4,116},{902,918},{6... | collective-permute-start | bytes 196616 | tf_op jit(solution)/shard_map/cond/branch_7_fun/ppermute | solution.py:102
  10.5 16.7 %collective-permute-start.73 = (f32[8,2,8,128]{3,2,1,0:T(8,128)S(1)}, f32[8,2,8,128]{3,2,1,0:T(8,128)S(1)}, u32[]{:S(2)}, u32[]{:S(2)}) collective-permute-start(f32[8,2,8,128]{3,2,1,0:T(8,128)S(1)} %get-tuple-element.698), channel_id=1, source_target_pairs={{896,910},{0,114},{898,912},{2,116},{900,914},{4,118},{902,916},{6... | collective-permute-start | bytes 196616 | tf_op jit(solution)/shard_map/cond/branch_7_fun/ppermute | solution.py:103
  27.2 4.3 %collective-permute-start.76 = (f32[8,8,128]{2,1,0:T(8,128)S(1)}, f32[8,8,128]{2,1,0:T(8,128)}, u32[]{:S(2)}, u32[]{:S(2)}) collective-permute-start(f32[8,8,128]{2,1,0:T(8,128)S(1)} %get-tuple-element.701), channel_id=1, source_target_pairs={{0,2},{2,4},{4,6},{6,8},{8,10},{10,12},{12,14},{14,16},{16,18},{18... | collective-permute-start | bytes 98312 | tf_op jit(solution)/shard_map/cond/branch_7_fun/ppermute | solution.py:108
  31.5 1.9 %collective-permute-start.77 = (f32[8,8,128]{2,1,0:T(8,128)S(1)}, f32[8,8,128]{2,1,0:T(8,128)}, u32[]{:S(2)}, u32[]{:S(2)}) collective-permute-start(f32[8,8,128]{2,1,0:T(8,128)S(1)} %get-tuple-element.702), channel_id=1, source_target_pairs={{2,0},{4,2},{6,4},{8,6},{10,8},{12,10},{14,12},{16,14},{18,16},{20... | collective-permute-start | bytes 98312 | tf_op jit(solution)/shard_map/cond/branch_7_fun/ppermute | solution.py:109
  33.5 5.0 %collective-permute-start.75 = (f32[8,4,128]{2,1,0:T(4,128)S(1)}, f32[8,4,128]{2,1,0:T(4,128)}, u32[]{:S(2)}, u32[]{:S(2)}) collective-permute-start(f32[8,4,128]{2,1,0:T(4,128)S(1)} %get-tuple-element.700), channel_id=1, source_target_pairs={{896,908},{0,116},{898,910},{2,118},{900,912},{4,120},{902,914},{6... | collective-permute-start | bytes 49160 | tf_op jit(solution)/shard_map/cond/branch_7_fun/ppermute | solution.py:104
  39.6 2.0 %collective-permute-done.75 = f32[8,4,128]{2,1,0:T(4,128)} collective-permute-done((f32[8,4,128]{2,1,0:T(4,128)S(1)}, f32[8,4,128]{2,1,0:T(4,128)}, u32[]{:S(2)}, u32[]{:S(2)}) %collective-permute-start.75) | collective-permute-done | bytes 16416 | tf_op jit(solution)/shard_map/cond/branch_7_fun/ppermute | solution.py:104
  46.0 24.7 %conditional.5 = (f32[8,2,8,128]{3,2,1,0:T(8,128)}, f32[8,2,8,128]{3,2,1,0:T(8,128)}) conditional(s32[]{:T(128)} %clamp.12, (pred[8,2,8,128]{3,2,1,0:T(8,128)(4,1)S(1)}, f32[8,2,8,128]{3,2,1,0:T(8,128)S(1)}, f32[8,2,8,128]{3,2,1,0:T(8,128)S(1)}, pred[]{:T(512)}, f32[8,2,8,128]{3,2,1,0:T(8,128)S(1)}) %tuple.254, ...), branch_computations={%region_8.9_spmd, %region_9.10_spmd, %region_10.11_spmd, %region_1... | conditional | flops 32768 | bytes 868449 | solution.py:159
  46.0 7.5 %collective-permute-start.8 = (f32[8,2,8,128]{3,2,1,0:T(8,128)S(1)}, f32[8,2,8,128]{3,2,1,0:T(8,128)}, u32[]{:S(2)}, u32[]{:S(2)}) collective-permute-start(f32[8,2,8,128]{3,2,1,0:T(8,128)S(1)} %get-tuple-element.908), channel_id=1, source_target_pairs={{0,128},{2,130},{4,132},{6,134},{8,136},{10,138},{12,140},{14,142}... | collective-permute-start | bytes 196616 | tf_op jit(solution)/shard_map/cond/branch_4_fun/ppermute | solution.py:120
  53.6 1.9 %collective-permute-start.9 = (f32[8,2,8,128]{3,2,1,0:T(8,128)S(1)}, f32[8,2,8,128]{3,2,1,0:T(8,128)}, u32[]{:S(2)}, u32[]{:S(2)}) collective-permute-start(f32[8,2,8,128]{3,2,1,0:T(8,128)S(1)} %get-tuple-element.907), channel_id=1, source_target_pairs={{128,0},{130,2},{132,4},{134,6},{136,8},{138,10},{140,12},{142,14}... | collective-permute-start | bytes 196616 | tf_op jit(solution)/shard_map/cond/branch_4_fun/ppermute | solution.py:120
  55.5 15.1 %collective-permute-done.9 = f32[8,2,8,128]{3,2,1,0:T(8,128)} collective-permute-done((f32[8,2,8,128]{3,2,1,0:T(8,128)S(1)}, f32[8,2,8,128]{3,2,1,0:T(8,128)}, u32[]{:S(2)}, u32[]{:S(2)}) %collective-permute-start.9) | collective-permute-done | bytes 65568 | tf_op jit(solution)/shard_map/cond/branch_4_fun/ppermute | solution.py:120
  77.6 36.6 %conditional.6 = (f32[8,2,8,128]{3,2,1,0:T(8,128)}, f32[8,2,8,128]{3,2,1,0:T(8,128)S(1)}, f32[8,4,8,128]{3,2,1,0:T(8,128)}, f32[8,2,2,128]{3,2,1,0:T(2,128)}, f3...) conditional(s32[]{:T(128)} %clamp.15, ...), branch_computations={%region_22.23_spmd, %region_23.24_spmd, %region_24.25_spmd, %regio... | conditional | bytes 1777996 | solution.py:138
  77.6 1.9 %collective-permute-start.85 = (f32[8,4,8,128]{3,2,1,0:T(8,128)S(1)}, f32[8,4,8,128]{3,2,1,0:T(8,128)}, u32[]{:S(2)}, u32[]{:S(2)}) collective-permute-start(f32[8,4,8,128]{3,2,1,0:T(8,128)S(1)} %get-tuple-element.749), channel_id=1, source_target_pairs={{0,1},{1,0},{2,3},{3,2},{4,5},{5,4},{6,7},{7,6},{8,9},{9,8},{10,11... | collective-permute-start | bytes 393224 | tf_op jit(solution)/shard_map/cond/branch_1_fun/ppermute | solution.py:105
  79.5 8.3 %collective-permute-start.83 = (f32[8,2,8,128]{3,2,1,0:T(8,128)S(1)}, f32[8,2,8,128]{3,2,1,0:T(8,128)S(1)}, u32[]{:S(2)}, u32[]{:S(2)}) collective-permute-start(f32[8,2,8,128]{3,2,1,0:T(8,128)S(1)} %get-tuple-element.748), channel_id=1, source_target_pairs={{896,900},{0,124},{898,902},{2,126},{900,904},{4,0},{902,906},{6,2... | collective-permute-start | bytes 196616 | tf_op jit(solution)/shard_map/cond/branch_1_fun/ppermute | solution.py:102
  87.8 16.4 %collective-permute-start.84 = (f32[8,2,8,128]{3,2,1,0:T(8,128)S(1)}, f32[8,2,8,128]{3,2,1,0:T(8,128)S(1)}, u32[]{:S(2)}, u32[]{:S(2)}) collective-permute-start(f32[8,2,8,128]{3,2,1,0:T(8,128)S(1)} %get-tuple-element.748), channel_id=1, source_target_pairs={{896,898},{0,126},{898,900},{2,0},{900,902},{4,2},{902,904},{6,4},... | collective-permute-start | bytes 196616 | tf_op jit(solution)/shard_map/cond/branch_1_fun/ppermute | solution.py:103
  104.2 1.9 %collective-permute-start.86 = (f32[8,8,128]{2,1,0:T(8,128)S(1)}, f32[8,8,128]{2,1,0:T(8,128)}, u32[]{:S(2)}, u32[]{:S(2)}) collective-permute-start(f32[8,8,128]{2,1,0:T(8,128)S(1)} %get-tuple-element.751), channel_id=1, source_target_pairs={{0,2},{2,4},{4,6},{6,8},{8,10},{10,12},{12,14},{14,16},{16,18},{18... | collective-permute-start | bytes 98312 | tf_op jit(solution)/shard_map/cond/branch_1_fun/ppermute | solution.py:108
  106.1 3.9 %collective-permute-start.87 = (f32[8,8,128]{2,1,0:T(8,128)S(1)}, f32[8,8,128]{2,1,0:T(8,128)}, u32[]{:S(2)}, u32[]{:S(2)}) collective-permute-start(f32[8,8,128]{2,1,0:T(8,128)S(1)} %get-tuple-element.752), channel_id=1, source_target_pairs={{2,0},{4,2},{6,4},{8,6},{10,8},{12,10},{14,12},{16,14},{18,16},{20... | collective-permute-start | bytes 98312 | tf_op jit(solution)/shard_map/cond/branch_1_fun/ppermute | solution.py:109
  111.8 2.4 %collective-permute-done.87 = f32[8,8,128]{2,1,0:T(8,128)} collective-permute-done((f32[8,8,128]{2,1,0:T(8,128)S(1)}, f32[8,8,128]{2,1,0:T(8,128)}, u32[]{:S(2)}, u32[]{:S(2)}) %collective-permute-start.87) | collective-permute-done | bytes 32800 | tf_op jit(solution)/shard_map/cond/branch_1_fun/ppermute | solution.py:109
  117.7 51.9 %conditional.7 = (f32[8,2,8,128]{3,2,1,0:T(8,128)}, f32[8,2,8,128]{3,2,1,0:T(8,128)}) conditional(s32[]{:T(128)} %clamp.14, (f32[8,2,8,128]{3,2,1,0:T(8,128)S(1)}, f32[]{:T(128)}, pred[8,2,8,128]{3,2,1,0:T(8,128)(4,1)S(1)}, f32[8,2,8,128]{3,2,1,0:T(8,128)S(1)}, pred[]{:T(512)}, ...), branch_computations={%region_30.31_spmd, %region_31.32_spmd, %region_32.33_spmd, %regio... | conditional | flops 36864 | bytes 909413 | solution.py:159
  117.8 26.9 %collective-permute-start.30 = (f32[8,2,8,128]{3,2,1,0:T(8,128)S(1)}, f32[8,2,8,128]{3,2,1,0:T(8,128)}, u32[]{:S(2)}, u32[]{:S(2)}) collective-permute-start(f32[8,2,8,128]{3,2,1,0:T(8,128)S(1)} %get-tuple-element.930), channel_id=1, source_target_pairs={{0,128},{2,130},{4,132},{6,134},{8,136},{10,138},{12,140},{14,142}... | collective-permute-start | bytes 196616 | tf_op jit(solution)/shard_map/cond/branch_7_fun/ppermute | solution.py:120
  144.8 1.9 %collective-permute-start.31 = (f32[8,2,8,128]{3,2,1,0:T(8,128)S(1)}, f32[8,2,8,128]{3,2,1,0:T(8,128)}, u32[]{:S(2)}, u32[]{:S(2)}) collective-permute-start(f32[8,2,8,128]{3,2,1,0:T(8,128)S(1)} %get-tuple-element.929), channel_id=1, source_target_pairs={{128,0},{130,2},{132,4},{134,6},{136,8},{138,10},{140,12},{142,14}... | collective-permute-start | bytes 196616 | tf_op jit(solution)/shard_map/cond/branch_7_fun/ppermute | solution.py:120
  147.3 22.4 %collective-permute-done.31 = f32[8,2,8,128]{3,2,1,0:T(8,128)} collective-permute-done((f32[8,2,8,128]{3,2,1,0:T(8,128)S(1)}, f32[8,2,8,128]{3,2,1,0:T(8,128)}, u32[]{:S(2)}, u32[]{:S(2)}) %collective-permute-start.31) | collective-permute-done | bytes 65568 | tf_op jit(solution)/shard_map/cond/branch_7_fun/ppermute | solution.py:120
  (119 shorter events, 18.7 us)
Async XLA Ops:
  0.0 2.0 %copy-start.18 = (f32[3,4,8,128]{3,2,1,0:T(8,128)S(1)}, f32[3,4,8,128]{3,2,1,0:T(8,128)}, u32[]{:S(2)}) copy-start(f32[3,4,8,128]{3,2,1,0:T(8,128)} %param.67) | copy-start | bytes 147460
  2.0 0.7 copy-start.1
  2.7 0.7 copy-start.19
  3.4 0.8 copy-start
  4.4 34.1 %collective-permute-start.74 = (f32[8,4,8,128]{3,2,1,0:T(8,128)S(1)}, f32[8,4,8,128]{3,2,1,0:T(8,128)}, u32[]{:S(2)}, u32[]{:S(2)}) collective-permute-start(f32[8,4,8,128]{3,2,1,0:T(8,128)S(1)} %get-tuple-element.699), channel_id=1, source_target_pairs={{0,1},{1,0},{2,3},{3,2},{4,5},{5,4},{6,7},{7,6},{8,9},{9,8},{10,11... | collective-permute-start | bytes 393224 | tf_op jit(solution)/shard_map/cond/branch_7_fun/ppermute | solution.py:105
  6.3 27.1 %collective-permute-start.72 = (f32[8,2,8,128]{3,2,1,0:T(8,128)S(1)}, f32[8,2,8,128]{3,2,1,0:T(8,128)S(1)}, u32[]{:S(2)}, u32[]{:S(2)}) collective-permute-start(f32[8,2,8,128]{3,2,1,0:T(8,128)S(1)} %get-tuple-element.698), channel_id=1, source_target_pairs={{896,912},{0,112},{898,914},{2,114},{900,916},{4,116},{902,918},{6... | collective-permute-start | bytes 196616 | tf_op jit(solution)/shard_map/cond/branch_7_fun/ppermute | solution.py:102
  10.5 27.9 %collective-permute-start.73 = (f32[8,2,8,128]{3,2,1,0:T(8,128)S(1)}, f32[8,2,8,128]{3,2,1,0:T(8,128)S(1)}, u32[]{:S(2)}, u32[]{:S(2)}) collective-permute-start(f32[8,2,8,128]{3,2,1,0:T(8,128)S(1)} %get-tuple-element.698), channel_id=1, source_target_pairs={{896,910},{0,114},{898,912},{2,116},{900,914},{4,118},{902,916},{6... | collective-permute-start | bytes 196616 | tf_op jit(solution)/shard_map/cond/branch_7_fun/ppermute | solution.py:103
  27.2 14.4 %collective-permute-start.76 = (f32[8,8,128]{2,1,0:T(8,128)S(1)}, f32[8,8,128]{2,1,0:T(8,128)}, u32[]{:S(2)}, u32[]{:S(2)}) collective-permute-start(f32[8,8,128]{2,1,0:T(8,128)S(1)} %get-tuple-element.701), channel_id=1, source_target_pairs={{0,2},{2,4},{4,6},{6,8},{8,10},{10,12},{12,14},{14,16},{16,18},{18... | collective-permute-start | bytes 98312 | tf_op jit(solution)/shard_map/cond/branch_7_fun/ppermute | solution.py:108
  31.5 10.1 %collective-permute-start.77 = (f32[8,8,128]{2,1,0:T(8,128)S(1)}, f32[8,8,128]{2,1,0:T(8,128)}, u32[]{:S(2)}, u32[]{:S(2)}) collective-permute-start(f32[8,8,128]{2,1,0:T(8,128)S(1)} %get-tuple-element.702), channel_id=1, source_target_pairs={{2,0},{4,2},{6,4},{8,6},{10,8},{12,10},{14,12},{16,14},{18,16},{20... | collective-permute-start | bytes 98312 | tf_op jit(solution)/shard_map/cond/branch_7_fun/ppermute | solution.py:109
  33.4 6.1 %copy-start.9 = (f32[8,2,8,128]{3,2,1,0:T(8,128)}, f32[8,2,8,128]{3,2,1,0:T(8,128)S(1)}, u32[]{:S(2)}) copy-start(f32[8,2,8,128]{3,2,1,0:T(8,128)S(1)} %collective-permute-done.72) | copy-start | bytes 196612 | tf_op jit(solution)/shard_map/cond
  33.5 8.1 %collective-permute-start.75 = (f32[8,4,128]{2,1,0:T(4,128)S(1)}, f32[8,4,128]{2,1,0:T(4,128)}, u32[]{:S(2)}, u32[]{:S(2)}) collective-permute-start(f32[8,4,128]{2,1,0:T(4,128)S(1)} %get-tuple-element.700), channel_id=1, source_target_pairs={{896,908},{0,116},{898,910},{2,118},{900,912},{4,120},{902,914},{6... | collective-permute-start | bytes 49160 | tf_op jit(solution)/shard_map/cond/branch_7_fun/ppermute | solution.py:104
  41.6 1.0 copy-start.20
  46.0 9.5 %collective-permute-start.8 = (f32[8,2,8,128]{3,2,1,0:T(8,128)S(1)}, f32[8,2,8,128]{3,2,1,0:T(8,128)}, u32[]{:S(2)}, u32[]{:S(2)}) collective-permute-start(f32[8,2,8,128]{3,2,1,0:T(8,128)S(1)} %get-tuple-element.908), channel_id=1, source_target_pairs={{0,128},{2,130},{4,132},{6,134},{8,136},{10,138},{12,140},{14,142}... | collective-permute-start | bytes 196616 | tf_op jit(solution)/shard_map/cond/branch_4_fun/ppermute | solution.py:120
  53.6 17.1 %collective-permute-start.9 = (f32[8,2,8,128]{3,2,1,0:T(8,128)S(1)}, f32[8,2,8,128]{3,2,1,0:T(8,128)}, u32[]{:S(2)}, u32[]{:S(2)}) collective-permute-start(f32[8,2,8,128]{3,2,1,0:T(8,128)S(1)} %get-tuple-element.907), channel_id=1, source_target_pairs={{128,0},{130,2},{132,4},{134,6},{136,8},{138,10},{140,12},{142,14}... | collective-permute-start | bytes 196616 | tf_op jit(solution)/shard_map/cond/branch_4_fun/ppermute | solution.py:120
  77.6 33.1 %collective-permute-start.85 = (f32[8,4,8,128]{3,2,1,0:T(8,128)S(1)}, f32[8,4,8,128]{3,2,1,0:T(8,128)}, u32[]{:S(2)}, u32[]{:S(2)}) collective-permute-start(f32[8,4,8,128]{3,2,1,0:T(8,128)S(1)} %get-tuple-element.749), channel_id=1, source_target_pairs={{0,1},{1,0},{2,3},{3,2},{4,5},{5,4},{6,7},{7,6},{8,9},{9,8},{10,11... | collective-permute-start | bytes 393224 | tf_op jit(solution)/shard_map/cond/branch_1_fun/ppermute | solution.py:105
  79.5 31.1 %collective-permute-start.83 = (f32[8,2,8,128]{3,2,1,0:T(8,128)S(1)}, f32[8,2,8,128]{3,2,1,0:T(8,128)S(1)}, u32[]{:S(2)}, u32[]{:S(2)}) collective-permute-start(f32[8,2,8,128]{3,2,1,0:T(8,128)S(1)} %get-tuple-element.748), channel_id=1, source_target_pairs={{896,900},{0,124},{898,902},{2,126},{900,904},{4,0},{902,906},{6,2... | collective-permute-start | bytes 196616 | tf_op jit(solution)/shard_map/cond/branch_1_fun/ppermute | solution.py:102
  87.8 22.8 %collective-permute-start.84 = (f32[8,2,8,128]{3,2,1,0:T(8,128)S(1)}, f32[8,2,8,128]{3,2,1,0:T(8,128)S(1)}, u32[]{:S(2)}, u32[]{:S(2)}) collective-permute-start(f32[8,2,8,128]{3,2,1,0:T(8,128)S(1)} %get-tuple-element.748), channel_id=1, source_target_pairs={{896,898},{0,126},{898,900},{2,0},{900,902},{4,2},{902,904},{6,4},... | collective-permute-start | bytes 196616 | tf_op jit(solution)/shard_map/cond/branch_1_fun/ppermute | solution.py:103
  104.2 7.6 %collective-permute-start.86 = (f32[8,8,128]{2,1,0:T(8,128)S(1)}, f32[8,8,128]{2,1,0:T(8,128)}, u32[]{:S(2)}, u32[]{:S(2)}) collective-permute-start(f32[8,8,128]{2,1,0:T(8,128)S(1)} %get-tuple-element.751), channel_id=1, source_target_pairs={{0,2},{2,4},{4,6},{6,8},{8,10},{10,12},{12,14},{14,16},{16,18},{18... | collective-permute-start | bytes 98312 | tf_op jit(solution)/shard_map/cond/branch_1_fun/ppermute | solution.py:108
  106.1 8.0 %collective-permute-start.87 = (f32[8,8,128]{2,1,0:T(8,128)S(1)}, f32[8,8,128]{2,1,0:T(8,128)}, u32[]{:S(2)}, u32[]{:S(2)}) collective-permute-start(f32[8,8,128]{2,1,0:T(8,128)S(1)} %get-tuple-element.752), channel_id=1, source_target_pairs={{2,0},{4,2},{6,4},{8,6},{10,8},{12,10},{14,12},{16,14},{18,16},{20... | collective-permute-start | bytes 98312 | tf_op jit(solution)/shard_map/cond/branch_1_fun/ppermute | solution.py:109
  110.6 1.1 copy-start.11
  117.8 29.4 %collective-permute-start.30 = (f32[8,2,8,128]{3,2,1,0:T(8,128)S(1)}, f32[8,2,8,128]{3,2,1,0:T(8,128)}, u32[]{:S(2)}, u32[]{:S(2)}) collective-permute-start(f32[8,2,8,128]{3,2,1,0:T(8,128)S(1)} %get-tuple-element.930), channel_id=1, source_target_pairs={{0,128},{2,130},{4,132},{6,134},{8,136},{10,138},{12,140},{14,142}... | collective-permute-start | bytes 196616 | tf_op jit(solution)/shard_map/cond/branch_7_fun/ppermute | solution.py:120
  144.8 24.9 %collective-permute-start.31 = (f32[8,2,8,128]{3,2,1,0:T(8,128)S(1)}, f32[8,2,8,128]{3,2,1,0:T(8,128)}, u32[]{:S(2)}, u32[]{:S(2)}) collective-permute-start(f32[8,2,8,128]{3,2,1,0:T(8,128)S(1)} %get-tuple-element.929), channel_id=1, source_target_pairs={{128,0},{130,2},{132,4},{134,6},{136,8},{138,10},{140,12},{142,14}... | collective-permute-start | bytes 196616 | tf_op jit(solution)/shard_map/cond/branch_7_fun/ppermute | solution.py:120
